TPU v7x, 32 devices: a whole 2x2x4 slice. The times are simulated.
32 devices in a mesh: chan: 16 (over z, y, core), day: 2 (over x).
Axes of the slice: x: 2, y: 2, z: 4, core: 2. Of those that a mesh axis runs over, the one named last changes fastest.
Arguments:
- spectra: bfloat16 [2, 256, 80, 256], P('day', 'chan'), may hold values from -500 to 500
Outputs:
- stacked: float32 [256, 256, 256], P('day', 'chan')
All inputs are finite; a program needn't handle non-finite values.
Results may differ from a plain program's by a relative error of at most 0.0023.
Values may be sent and summed in bfloat16 or wider, within the bound.
No kernel may reach another device: no remote copies, remote signals or barrier semaphores. Data moves between devices by JAX's collectives and lax.ppermute only.
A program may use at most 128 MiB of HBM per device.

v0:
```python
import functools

import jax
import jax.numpy as jnp
import numpy as np
from jax import lax
from jax.experimental import pallas as pl
from jax.experimental.pallas import tpu as pltpu
from jax.sharding import PartitionSpec as P

VMEM_LIMIT = 48 * 1024 * 1024
PACK_VMEM_LIMIT = 53 * 1024 * 1024
FETCHES = 4
SENDS = 2
TALL = 2


def freq_taper(bins):
    freq_index = jnp.arange(bins, dtype=jnp.float32)
    half_taper = 0.54 - 0.46 * jnp.cos(2.0 * jnp.pi * (freq_index + 0.5) / bins)
    return jnp.concatenate([half_taper, half_taper])


def whiten(spectra):
    values = spectra.astype(jnp.float32)
    bins = values.shape[-1] // 2
    band_power = jnp.sum(values * values, axis=-1, keepdims=True) / bins + 1e-06
    return (values * freq_taper(bins) / jnp.sqrt(band_power)).astype(jnp.bfloat16)


def lag_matrix(bins):
    lag_count = 2 * bins
    freq_index = jnp.arange(bins, dtype=jnp.int32)
    lag_index = jnp.arange(lag_count, dtype=jnp.int32) - bins
    wound = jnp.mod(freq_index[:, None] * lag_index[None, :], lag_count)
    phase_angle = 2.0 * jnp.pi / lag_count * wound.astype(jnp.float32)
    return jnp.concatenate([jnp.cos(phase_angle), -jnp.sin(phase_angle)], axis=0)


def cross_spectra(far_rows, near_rows):
    bins = far_rows.shape[-1] // 2
    windows = far_rows.shape[-2]
    far_re, far_im = (far_rows[..., :bins], far_rows[..., bins:])
    near_re, near_im = (near_rows[..., :bins], near_rows[..., bins:])
    real_part = jnp.einsum("jwf,iwf->jif", far_re, near_re, preferred_element_type=jnp.float32)
    real_part = real_part + jnp.einsum(
        "jwf,iwf->jif", far_im, near_im, preferred_element_type=jnp.float32
    )
    imag_part = jnp.einsum("jwf,iwf->jif", far_re, near_im, preferred_element_type=jnp.float32)
    imag_part = imag_part - jnp.einsum(
        "jwf,iwf->jif", far_im, near_re, preferred_element_type=jnp.float32
    )
    return jnp.concatenate([real_part, imag_part], axis=-1) / windows


def to_lags(cross, table):
    flat = cross.reshape(-1, cross.shape[-1])
    lagged = jnp.dot(
        flat, table, precision=lax.Precision.HIGHEST, preferred_element_type=jnp.float32
    )
    return lagged.reshape(cross.shape[:-1] + (table.shape[1],))


def gathered_shards(spectra):
    local_white = whiten(spectra)[0]
    gathered = lax.all_gather(local_white, "chan", axis=0, tiled=True)
    table = lag_matrix(local_white.shape[-1] // 2)
    day_count = lax.axis_size("day")
    return lax.psum_scatter(
        to_lags(cross_spectra(gathered, local_white), table) / day_count,
        "day",
        scatter_dimension=0,
        tiled=True,
    )


def lag_table(bins, per_dev, groups, scale):
    lags = 2 * bins
    freq = (np.arange(per_dev)[None, :] * groups + np.arange(groups)[:, None]).reshape(-1)
    wound = (freq[:, None] * (np.arange(lags)[None, :] - bins)) % lags
    angle = 2.0 * np.pi / lags * wound
    table = (np.stack([np.cos(angle), -np.sin(angle)], axis=1) * scale).reshape(2 * bins, lags)
    table = table.astype(np.float32)
    high = table.astype(jnp.bfloat16)
    low = (table - high.astype(np.float32)).astype(jnp.bfloat16)
    return high, low


def pack_kernel(groups, per_dev, spectra_ref, out_ref, held_ref, rows_ref, arrived):
    chans, windows, width = held_ref.shape
    bins = width // 2
    head = bins // 2
    size = (per_dev + 1) * chans
    stride = size + 1
    fetches = arrived.shape[0]
    batch = chans // fetches
    copies = []
    for step in range(fetches):
        part = pl.ds(step * batch, batch)
        copies.append(pltpu.make_async_copy(spectra_ref.at[part], held_ref.at[part], arrived.at[step]))
        copies[-1].start()
    freq = (lax.broadcasted_iota(jnp.int32, (1, width), 1) % bins).astype(jnp.float32)
    taper = 0.54 - 0.46 * jnp.cos(2.0 * jnp.pi * (freq + 0.5) / bins)
    lane = lax.broadcasted_iota(jnp.int32, (windows - head, bins), 1)
    pick = lax.broadcasted_iota(jnp.int32, (groups, bins), 1) % groups
    pick = (pick == lax.broadcasted_iota(jnp.int32, (groups, bins), 0)).astype(jnp.float32).astype(jnp.bfloat16)

    def whiten_channel(ch):
        values = held_ref[ch].astype(jnp.float32)
        power = jnp.sum(values * values, axis=-1, keepdims=True) / bins + 1e-06
        return (values * taper * lax.rsqrt(power)).astype(jnp.bfloat16)

    def place_channel(ch, white):
        real, imag = white[:, :bins], white[:, bins:]
        main = jnp.concatenate([real[:head], imag[:head]], axis=0).astype(jnp.float32).T
        spread = []
        for slot in range(per_dev):
            chosen = lane // groups == slot
            spread += [jnp.where(chosen, part[head:], jnp.zeros_like(part[head:])) for part in (real, imag)]
        tail = lax.dot_general(
            pick, jnp.concatenate(spread, axis=0), (((1,), (1,)), ((), ())), preferred_element_type=jnp.float32
        )
        for slot in range(per_dev):
            part = main[slot * groups:(slot + 1) * groups]
            rows_ref[pl.ds(slot * chans + ch, groups, stride=stride), :] = part
        rows_ref[pl.ds(per_dev * chans + ch, groups, stride=stride), :] = tail

    ready = []
    for step in range(fetches):
        copies[step].wait()
        fresh = [(ch, whiten_channel(ch)) for ch in range(step * batch, (step + 1) * batch)]
        for ch, white in ready:
            place_channel(ch, white)
        ready = fresh
    for ch, white in ready:
        place_channel(ch, white)
    for group in range(groups):
        rows = rows_ref[pl.ds(group * stride, size), :]
        out_ref[group] = rows.astype(jnp.bfloat16).reshape(out_ref.shape[1:])


def swap_parts(rows, half):
    lanes = rows.shape[-1]
    values = rows.astype(jnp.float32)
    lane = lax.broadcasted_iota(jnp.int32, values.shape, 1)
    first = (lane % (2 * half)) < half
    ahead = pltpu.roll(values, lanes - half, 1)
    behind = pltpu.roll(values, half, 1)
    return jnp.where(first, ahead, -behind).astype(jnp.bfloat16)


def cross_kernel(order, days, in_ref, out_ref):
    groups, parts, chans, lanes = in_ref.shape
    blocks = groups // days
    per_dev = parts - 1
    total = blocks * chans
    far = out_ref.shape[-1]
    narrow = lanes // per_dev // 2

    def rows(day, part):
        return jnp.concatenate([in_ref[order[block][day], part] for block in range(blocks)], axis=0)

    tails = [rows(day, per_dev) for day in range(days)]
    tails_swapped = [swap_parts(tail, narrow) for tail in tails]
    far_tail = jnp.concatenate(tails, axis=1)
    lane = lax.broadcasted_iota(jnp.int32, (2 * total, lanes), 1) // (2 * narrow)
    dims = (((1,), (1,)), ((), ()))
    for slot in range(per_dev):
        mains = [rows(day, slot) for day in range(days)]
        far_main = jnp.concatenate(mains, axis=1)
        turned = [swap_parts(m, lanes // 2) for m in mains]
        near_main = [jnp.concatenate(pair, axis=0) for pair in zip(mains, turned)]
        near_tail = [jnp.concatenate(pair, axis=0) for pair in zip(tails, tails_swapped)]
        near_tail = [jnp.where(lane == slot, t, jnp.zeros_like(t)) for t in near_tail]
        cross = lax.dot_general(
            jnp.concatenate(near_main, axis=1), far_main, dims, preferred_element_type=jnp.float32
        ) + lax.dot_general(
            jnp.concatenate(near_tail, axis=1), far_tail, dims, preferred_element_type=jnp.float32
        )
        cross = cross.astype(out_ref.dtype)
        for kind in range(2):
            for block in range(blocks):
                start = kind * total + block * chans
                for half in range(days):
                    piece = cross[start:start + chans, half * far:(half + 1) * far]
                    out_ref[order[block][half], 2 * slot + kind] = piece


def lags_kernel(cross_ref, high_ref, low_ref, out_ref, rows_ref, lag_ref, sent):
    far, chans, _ = out_ref.shape
    depth = high_ref.shape[0]
    stride = chans + 1
    for row in range(depth):
        rows_ref[pl.ds(row * stride, chans), :] = cross_ref[pl.ds(row * chans, chans), :].astype(jnp.float32)
    high, low = high_ref[...], low_ref[...]
    dims = (((0,), (0,)), ((), ()))
    parts = sent.shape[0]
    batch = chans // parts
    copies = []
    for step in range(parts):
        for first in range(step * batch, (step + 1) * batch, TALL):
            group = range(first, first + TALL)
            part = [rows_ref[pl.ds(ch, depth, stride=stride), :].astype(jnp.bfloat16) for ch in group]
            part = jnp.concatenate(part, axis=1)
            lag = lax.dot_general(part, high, dims, preferred_element_type=jnp.float32)
            lag = lag + lax.dot_general(part, low, dims, preferred_element_type=jnp.float32)
            for place, ch in enumerate(group):
                lag_ref[:, ch, :] = lag[place * far:(place + 1) * far]
        done = pl.ds(step * batch, batch)
        copies.append(pltpu.make_async_copy(lag_ref.at[:, done], out_ref.at[:, done], sent.at[step]))
        copies[-1].start()
    for copy in copies:
        copy.wait()


def call(kernel, out_shape, scratch, in_spaces, out_space, *operands, vmem=VMEM_LIMIT):
    return pl.pallas_call(
        kernel,
        out_shape=out_shape,
        in_specs=[pl.BlockSpec(memory_space=space) for space in in_spaces],
        out_specs=pl.BlockSpec(memory_space=out_space),
        scratch_shapes=scratch,
        compiler_params=pltpu.CompilerParams(vmem_limit_bytes=vmem),
    )(*operands)


def shards(axes, order, spectra):
    _, chans, windows, width = spectra.shape
    bins = width // 2
    n_chan, n_day = order.shape
    groups = n_chan * n_day
    per_dev = bins // groups
    far = n_chan * chans // n_day

    packed = call(
        functools.partial(pack_kernel, groups, per_dev),
        jax.ShapeDtypeStruct((groups, per_dev + 1, chans, bins), jnp.bfloat16),
        [
            pltpu.VMEM((chans, windows, width), jnp.bfloat16),
            pltpu.VMEM((groups * ((per_dev + 1) * chans + 1), bins), jnp.float32),
            pltpu.SemaphoreType.DMA((FETCHES,)),
        ],
        [pltpu.HBM],
        pltpu.VMEM,
        spectra[0],
        vmem=PACK_VMEM_LIMIT,
    )
    mine = lax.all_to_all(packed, axes, 0, 0, tiled=True)
    cross = call(
        functools.partial(cross_kernel, order.tolist(), n_day),
        jax.ShapeDtypeStruct((groups, 2 * per_dev, chans, far), jnp.bfloat16),
        [],
        [pltpu.VMEM],
        pltpu.VMEM,
        mine,
    )
    cross = lax.all_to_all(cross, axes, 0, 0, tiled=True)
    high, low = lag_table(bins, per_dev, groups, 1.0 / (windows * n_day))
    return call(
        lags_kernel,
        jax.ShapeDtypeStruct((far, chans, width), jnp.float32),
        [
            pltpu.VMEM((width * (chans + 1), far), jnp.float32),
            pltpu.VMEM((far, chans, width), jnp.float32),
            pltpu.SemaphoreType.DMA((SENDS,)),
        ],
        [pltpu.VMEM] * 3,
        pltpu.HBM,
        cross.reshape(width * chans, far),
        jnp.asarray(high),
        jnp.asarray(low),
    )


def solution(mesh):
    n_chan, n_day = mesh.shape["chan"], mesh.shape["day"]
    outer = 4 if n_chan % 4 == 0 else 1
    inner = n_chan // outer
    split_mesh = jax.sharding.Mesh(mesh.devices.reshape(outer, inner, n_day), ("outer", "inner", "day"))
    order = np.arange(n_chan * n_day).reshape(n_day, inner, outer).transpose(2, 1, 0).reshape(n_chan, n_day)

    def run(spectra):
        bins = spectra.shape[-1] // 2
        if bins % (n_chan * n_day):
            return jax.shard_map(
                gathered_shards,
                mesh=mesh,
                in_specs=(P("day", "chan", None, None),),
                out_specs=P("day", "chan", None),
                check_vma=False,
            )(spectra)
        return jax.shard_map(
            functools.partial(shards, ("day", "inner", "outer"), order),
            mesh=split_mesh,
            in_specs=(P("day", ("outer", "inner"), None, None),),
            out_specs=P("day", ("outer", "inner"), None),
            check_vma=False,
        )(spectra)

    return run
```

profile of v0, /device:TPU:1, one launch (start us, length us, event | category | flops | bytes accessed | tf_op | source)
XLA Modules:
  0.0 59.1 jit_solution(168972056032796501)
XLA Ops:
  0.0 1.7 %shard_map.37 = bf16[32,5,16,128]{3,2,1,0:T(8,128)(2,1)S(1)} custom-call(bf16[16,80,256]{2,1,0:T(8,128)(2,1)} %bitcast.3), custom_call_target="tpu_custom_call" | custom-call | tf_op jit(solution)/shard_map/pallas_call | solution.py:217
  1.8 25.0 %all_to_all.10.in_ref = bf16[32,5,16,128]{3,2,1,0:T(8,128)(2,1)S(1)} all-to-all(bf16[32,5,16,128]{3,2,1,0:T(8,128)(2,1)S(1)} %shard_map.37), channel_id=1, replica_groups=mesh['outer'=4,'inner'=4,'day'=2] {'day','inner','outer'}, dimensions={0} | all-to-all | bytes 1310720 | tf_op jit(solution)/shard_map/all_to_all | solution.py:248
  26.7 0.0 copy-start
  26.7 0.0 copy-start.1
  26.7 0.7 %shard_map.38 = bf16[32,8,16,128]{3,2,1,0:T(8,128)(2,1)S(1)} custom-call(bf16[32,5,16,128]{3,2,1,0:T(8,128)(2,1)S(1)} %all_to_all.10.in_ref), custom_call_target="tpu_custom_call" | custom-call | tf_op jit(solution)/shard_map/pallas_call | solution.py:217
  27.5 29.3 %all_to_all.11 = bf16[32,8,16,128]{3,2,1,0:T(8,128)(2,1)S(1)} all-to-all(bf16[32,8,16,128]{3,2,1,0:T(8,128)(2,1)S(1)} %shard_map.38), channel_id=1, replica_groups=mesh['outer'=4,'inner'=4,'day'=2] {'day','inner','outer'}, dimensions={0} | all-to-all | bytes 2097152 | tf_op jit(solution)/shard_map/all_to_all | solution.py:257
  56.8 0.0 copy-done
  56.8 0.0 copy-done.1
  56.8 2.3 %shard_map.39 = f32[128,16,256]{2,1,0:T(8,128)} custom-call(bf16[4096,128]{1,0:T(8,128)(2,1)S(1)} %bitcast.2, bf16[256,256]{1,0:T(8,128)(2,1)S(1)} %copy-done.1, bf16[256,256]{1,0:T(8,128)(2,1)S(1)} %copy-done), custom_call_target="tpu_custom_call" | custom-call | tf_op jit(solution)/shard_map/pallas_call | solution.py:217
Async XLA Ops:
  26.7 30.1 %copy-start = (bf16[256,256]{1,0:T(8,128)(2,1)S(1)}, bf16[256,256]{1,0:T(8,128)(2,1)}, u32[]{:S(2)}) copy-start(bf16[256,256]{1,0:T(8,128)(2,1)} %constant.5.clone.low_ref) | copy-start | bytes 393220
  26.7 30.1 %copy-start.1 = (bf16[256,256]{1,0:T(8,128)(2,1)S(1)}, bf16[256,256]{1,0:T(8,128)(2,1)}, u32[]{:S(2)}) copy-start(bf16[256,256]{1,0:T(8,128)(2,1)} %constant.4.clone.high_ref) | copy-start | bytes 393220
where the time goes:
time: 59.3 us; the launch traced here: 59.1 us
  blocking collectives  54.3 us (92%)
  Pallas kernels  4.75 us (8%)
    all_to_all x1, blocking collectives, shards(): cross = lax.all_to_all(cross, axes, 0, 0, tiled=True)  29.3 us
    all_to_all x1, blocking collectives, shards(): mine = lax.all_to_all(packed, axes, 0, 0, tiled=True)  25 us
    pallas_call x3, Pallas kernels, call(): pl.pallas_call(kernel, out_shape=out_shape, in_specs=[pl.BlockSpec(memory...  4.75 us

commit v1 on v0

--- a/solution.py
+++ b/solution.py
@@ -12,7 +12,6 @@
 PACK_VMEM_LIMIT = 53 * 1024 * 1024
 FETCHES = 4
 SENDS = 2
-TALL = 2
 
 
 def freq_taper(bins):
@@ -187,25 +186,30 @@
 
 
 def lags_kernel(cross_ref, high_ref, low_ref, out_ref, rows_ref, lag_ref, sent):
-    far, chans, _ = out_ref.shape
+    chans = out_ref.shape[1]
     depth = high_ref.shape[0]
-    stride = chans + 1
-    for row in range(depth):
-        rows_ref[pl.ds(row * stride, chans), :] = cross_ref[pl.ds(row * chans, chans), :].astype(jnp.float32)
     high, low = high_ref[...], low_ref[...]
     dims = (((0,), (0,)), ((), ()))
     parts = sent.shape[0]
     batch = chans // parts
+    stride = batch + 1
+    share = depth // batch
+
+    def fill(step, rows):
+        for row in rows:
+            values = cross_ref[pl.ds(row * chans, chans), :].astype(jnp.float32)
+            rows_ref[step, pl.ds(row * stride, batch), :] = values[step * batch:(step + 1) * batch]
+
+    fill(0, range(depth))
     copies = []
     for step in range(parts):
-        for first in range(step * batch, (step + 1) * batch, TALL):
-            group = range(first, first + TALL)
-            part = [rows_ref[pl.ds(ch, depth, stride=stride), :].astype(jnp.bfloat16) for ch in group]
-            part = jnp.concatenate(part, axis=1)
+        for place in range(batch):
+            part = rows_ref[step, pl.ds(place, depth, stride=stride), :].astype(jnp.bfloat16)
+            if step + 1 < parts:
+                fill(step + 1, range(place * share, (place + 1) * share))
             lag = lax.dot_general(part, high, dims, preferred_element_type=jnp.float32)
             lag = lag + lax.dot_general(part, low, dims, preferred_element_type=jnp.float32)
-            for place, ch in enumerate(group):
-                lag_ref[:, ch, :] = lag[place * far:(place + 1) * far]
+            lag_ref[:, step * batch + place, :] = lag
         done = pl.ds(step * batch, batch)
         copies.append(pltpu.make_async_copy(lag_ref.at[:, done], out_ref.at[:, done], sent.at[step]))
         copies[-1].start()
@@ -260,7 +264,7 @@
         lags_kernel,
         jax.ShapeDtypeStruct((far, chans, width), jnp.float32),
         [
-            pltpu.VMEM((width * (chans + 1), far), jnp.float32),
+            pltpu.VMEM((SENDS, width * (chans // SENDS + 1), far), jnp.float32),
             pltpu.VMEM((far, chans, width), jnp.float32),
             pltpu.SemaphoreType.DMA((SENDS,)),
         ],

time: 59.3 us -> 59.2 us (level)
  no operation moved by 1% of the time
where the time goes in v1:
time: 59.2 us; the launch traced here: 59 us
  blocking collectives  54.3 us (92%)
  Pallas kernels  4.7 us (8%)
    all_to_all x1, blocking collectives, shards(): cross = lax.all_to_all(cross, axes, 0, 0, tiled=True)  29.3 us
    all_to_all x1, blocking collectives, shards(): mine = lax.all_to_all(packed, axes, 0, 0, tiled=True)  25 us
    pallas_call x3, Pallas kernels, call(): pl.pallas_call(kernel, out_shape=out_shape, in_specs=[pl.BlockSpec(memory...  4.7 us

profile of v1, /device:TPU:1, one launch (start us, length us, event | category | flops | bytes accessed | tf_op | source)
XLA Modules:
  0.0 59.0 jit_solution(715681329910582143)
XLA Ops:
  0.0 1.7 %shard_map.37 = bf16[32,5,16,128]{3,2,1,0:T(8,128)(2,1)S(1)} custom-call(bf16[16,80,256]{2,1,0:T(8,128)(2,1)} %bitcast.3), custom_call_target="tpu_custom_call" | custom-call | tf_op jit(solution)/shard_map/pallas_call | solution.py:221
  1.8 25.0 %all_to_all.10.in_ref = bf16[32,5,16,128]{3,2,1,0:T(8,128)(2,1)S(1)} all-to-all(bf16[32,5,16,128]{3,2,1,0:T(8,128)(2,1)S(1)} %shard_map.37), channel_id=1, replica_groups=mesh['outer'=4,'inner'=4,'day'=2] {'day','inner','outer'}, dimensions={0} | all-to-all | bytes 1310720 | tf_op jit(solution)/shard_map/all_to_all | solution.py:252
  26.7 0.0 copy-start
  26.7 0.0 copy-start.1
  26.7 0.7 %shard_map.38 = bf16[32,8,16,128]{3,2,1,0:T(8,128)(2,1)S(1)} custom-call(bf16[32,5,16,128]{3,2,1,0:T(8,128)(2,1)S(1)} %all_to_all.10.in_ref), custom_call_target="tpu_custom_call" | custom-call | tf_op jit(solution)/shard_map/pallas_call | solution.py:221
  27.5 29.3 %all_to_all.11 = bf16[32,8,16,128]{3,2,1,0:T(8,128)(2,1)S(1)} all-to-all(bf16[32,8,16,128]{3,2,1,0:T(8,128)(2,1)S(1)} %shard_map.38), channel_id=1, replica_groups=mesh['outer'=4,'inner'=4,'day'=2] {'day','inner','outer'}, dimensions={0} | all-to-all | bytes 2097152 | tf_op jit(solution)/shard_map/all_to_all | solution.py:261
  56.8 0.0 copy-done
  56.8 0.0 copy-done.1
  56.8 2.2 %shard_map.39 = f32[128,16,256]{2,1,0:T(8,128)} custom-call(bf16[4096,128]{1,0:T(8,128)(2,1)S(1)} %bitcast.2, bf16[256,256]{1,0:T(8,128)(2,1)S(1)} %copy-done.1, bf16[256,256]{1,0:T(8,128)(2,1)S(1)} %copy-done), custom_call_target="tpu_custom_call" | custom-call | tf_op jit(solution)/shard_map/pallas_call | solution.py:221
Async XLA Ops:
  26.7 30.1 %copy-start = (bf16[256,256]{1,0:T(8,128)(2,1)S(1)}, bf16[256,256]{1,0:T(8,128)(2,1)}, u32[]{:S(2)}) copy-start(bf16[256,256]{1,0:T(8,128)(2,1)} %constant.5.clone.low_ref) | copy-start | bytes 393220
  26.7 30.1 %copy-start.1 = (bf16[256,256]{1,0:T(8,128)(2,1)S(1)}, bf16[256,256]{1,0:T(8,128)(2,1)}, u32[]{:S(2)}) copy-start(bf16[256,256]{1,0:T(8,128)(2,1)} %constant.4.clone.high_ref) | copy-start | bytes 393220

commit v2 on v1

--- a/solution.py
+++ b/solution.py
@@ -10,7 +10,7 @@
 
 VMEM_LIMIT = 48 * 1024 * 1024
 PACK_VMEM_LIMIT = 53 * 1024 * 1024
-FETCHES = 4
+FETCHES = 8
 SENDS = 2
 
 
@@ -189,7 +189,10 @@
     chans = out_ref.shape[1]
     depth = high_ref.shape[0]
     high, low = high_ref[...], low_ref[...]
-    dims = (((0,), (0,)), ((), ()))
+    far = cross_ref.shape[-1]
+    same = lax.broadcasted_iota(jnp.int32, (far, far), 0) == lax.broadcasted_iota(jnp.int32, (far, far), 1)
+    same = same.astype(jnp.float32).astype(jnp.bfloat16)
+    dims = (((1,), (1,)), ((), ()))
     parts = sent.shape[0]
     batch = chans // parts
     stride = batch + 1
@@ -207,8 +210,9 @@
             part = rows_ref[step, pl.ds(place, depth, stride=stride), :].astype(jnp.bfloat16)
             if step + 1 < parts:
                 fill(step + 1, range(place * share, (place + 1) * share))
-            lag = lax.dot_general(part, high, dims, preferred_element_type=jnp.float32)
-            lag = lag + lax.dot_general(part, low, dims, preferred_element_type=jnp.float32)
+            part = lax.dot_general(same, part, dims, preferred_element_type=jnp.float32).astype(jnp.bfloat16)
+            lag = jnp.dot(part, high, preferred_element_type=jnp.float32)
+            lag = lag + jnp.dot(part, low, preferred_element_type=jnp.float32)
             lag_ref[:, step * batch + place, :] = lag
         done = pl.ds(step * batch, batch)
         copies.append(pltpu.make_async_copy(lag_ref.at[:, done], out_ref.at[:, done], sent.at[step]))

time: 59.2 us -> 60.8 us (1.027)
  Pallas kernels: 4.7 us -> 6.25 us
    pallas_call x3, Pallas kernels: 4.7 us -> 6.25 us  [call(): pl.pallas_call(kernel, out_shape=out_shape, in_specs=[pl.BlockSpec(memory...]
where the time goes in v2:
time: 60.8 us; the launch traced here: 60.6 us
  blocking collectives  54.3 us (89%)
  Pallas kernels  6.25 us (10%)
    all_to_all x1, blocking collectives, shards(): cross = lax.all_to_all(cross, axes, 0, 0, tiled=True)  29.3 us
    all_to_all x1, blocking collectives, shards(): mine = lax.all_to_all(packed, axes, 0, 0, tiled=True)  25 us
    pallas_call x3, Pallas kernels, call(): pl.pallas_call(kernel, out_shape=out_shape, in_specs=[pl.BlockSpec(memory...  6.25 us

profile of v2, /device:TPU:1, one launch (start us, length us, event | category | flops | bytes accessed | tf_op | source)
XLA Modules:
  0.0 60.6 jit_solution(10011138349251516854)
XLA Ops:
  0.0 2.2 %shard_map.37 = bf16[32,5,16,128]{3,2,1,0:T(8,128)(2,1)S(1)} custom-call(bf16[16,80,256]{2,1,0:T(8,128)(2,1)} %bitcast.3), custom_call_target="tpu_custom_call" | custom-call | tf_op jit(solution)/shard_map/pallas_call | solution.py:225
  2.3 25.0 %all_to_all.10.in_ref = bf16[32,5,16,128]{3,2,1,0:T(8,128)(2,1)S(1)} all-to-all(bf16[32,5,16,128]{3,2,1,0:T(8,128)(2,1)S(1)} %shard_map.37), channel_id=1, replica_groups=mesh['outer'=4,'inner'=4,'day'=2] {'day','inner','outer'}, dimensions={0} | all-to-all | bytes 1310720 | tf_op jit(solution)/shard_map/all_to_all | solution.py:256
  27.2 0.0 copy-start
  27.2 0.0 copy-start.1
  27.2 0.7 %shard_map.38 = bf16[32,8,16,128]{3,2,1,0:T(8,128)(2,1)S(1)} custom-call(bf16[32,5,16,128]{3,2,1,0:T(8,128)(2,1)S(1)} %all_to_all.10.in_ref), custom_call_target="tpu_custom_call" | custom-call | tf_op jit(solution)/shard_map/pallas_call | solution.py:225
  28.0 29.3 %all_to_all.11 = bf16[32,8,16,128]{3,2,1,0:T(8,128)(2,1)S(1)} all-to-all(bf16[32,8,16,128]{3,2,1,0:T(8,128)(2,1)S(1)} %shard_map.38), channel_id=1, replica_groups=mesh['outer'=4,'inner'=4,'day'=2] {'day','inner','outer'}, dimensions={0} | all-to-all | bytes 2097152 | tf_op jit(solution)/shard_map/all_to_all | solution.py:265
  57.3 0.0 copy-done
  57.3 0.0 copy-done.1
  57.3 3.3 %shard_map.39 = f32[128,16,256]{2,1,0:T(8,128)} custom-call(bf16[4096,128]{1,0:T(8,128)(2,1)S(1)} %bitcast.2, bf16[256,256]{1,0:T(8,128)(2,1)S(1)} %copy-done.1, bf16[256,256]{1,0:T(8,128)(2,1)S(1)} %copy-done), custom_call_target="tpu_custom_call" | custom-call | tf_op jit(solution)/shard_map/pallas_call | solution.py:225
Async XLA Ops:
  27.2 30.1 %copy-start = (bf16[256,256]{1,0:T(8,128)(2,1)S(1)}, bf16[256,256]{1,0:T(8,128)(2,1)}, u32[]{:S(2)}) copy-start(bf16[256,256]{1,0:T(8,128)(2,1)} %constant.5.clone.low_ref) | copy-start | bytes 393220
  27.2 30.1 %copy-start.1 = (bf16[256,256]{1,0:T(8,128)(2,1)S(1)}, bf16[256,256]{1,0:T(8,128)(2,1)}, u32[]{:S(2)}) copy-start(bf16[256,256]{1,0:T(8,128)(2,1)} %constant.4.clone.high_ref) | copy-start | bytes 393220

commit v3 on v0

--- a/solution.py
+++ b/solution.py
@@ -10,9 +10,8 @@
 
 VMEM_LIMIT = 48 * 1024 * 1024
 PACK_VMEM_LIMIT = 53 * 1024 * 1024
-FETCHES = 4
+FETCHES = 2
 SENDS = 2
-TALL = 2
 
 
 def freq_taper(bins):
@@ -134,9 +133,10 @@
         ready = fresh
     for ch, white in ready:
         place_channel(ch, white)
-    for group in range(groups):
-        rows = rows_ref[pl.ds(group * stride, size), :]
-        out_ref[group] = rows.astype(jnp.bfloat16).reshape(out_ref.shape[1:])
+    for first in range(0, groups, 4):
+        rows = [rows_ref[pl.ds(group * stride, size), :].astype(jnp.bfloat16) for group in range(first, first + 4)]
+        for place, part in enumerate(rows):
+            out_ref[first + place] = part.reshape(out_ref.shape[1:])
 
 
 def swap_parts(rows, half):
@@ -187,28 +187,37 @@
 
 
 def lags_kernel(cross_ref, high_ref, low_ref, out_ref, rows_ref, lag_ref, sent):
-    far, chans, _ = out_ref.shape
+    chans = out_ref.shape[1]
     depth = high_ref.shape[0]
-    stride = chans + 1
-    for row in range(depth):
-        rows_ref[pl.ds(row * stride, chans), :] = cross_ref[pl.ds(row * chans, chans), :].astype(jnp.float32)
     high, low = high_ref[...], low_ref[...]
     dims = (((0,), (0,)), ((), ()))
     parts = sent.shape[0]
     batch = chans // parts
+    stride = chans + 1
+    for row in range(depth):
+        rows_ref[pl.ds(row * stride, chans), :] = cross_ref[pl.ds(row * chans, chans), :].astype(jnp.float32)
     copies = []
-    for step in range(parts):
-        for first in range(step * batch, (step + 1) * batch, TALL):
-            group = range(first, first + TALL)
-            part = [rows_ref[pl.ds(ch, depth, stride=stride), :].astype(jnp.bfloat16) for ch in group]
-            part = jnp.concatenate(part, axis=1)
-            lag = lax.dot_general(part, high, dims, preferred_element_type=jnp.float32)
-            lag = lag + lax.dot_general(part, low, dims, preferred_element_type=jnp.float32)
-            for place, ch in enumerate(group):
-                lag_ref[:, ch, :] = lag[place * far:(place + 1) * far]
-        done = pl.ds(step * batch, batch)
-        copies.append(pltpu.make_async_copy(lag_ref.at[:, done], out_ref.at[:, done], sent.at[step]))
-        copies[-1].start()
+
+    def load(ch):
+        return rows_ref[pl.ds(ch, depth, stride=stride), :].astype(jnp.bfloat16)
+
+    def store(ch, lag):
+        lag_ref[:, ch, :] = lag
+        if (ch + 1) % batch == 0:
+            step = ch // batch
+            done = pl.ds(step * batch, batch)
+            copies.append(pltpu.make_async_copy(lag_ref.at[:, done], out_ref.at[:, done], sent.at[step]))
+            copies[-1].start()
+
+    part, lag = load(0), None
+    for ch in range(chans):
+        following = load(ch + 1) if ch + 1 < chans else None
+        fresh = lax.dot_general(part, high, dims, preferred_element_type=jnp.float32)
+        fresh = fresh + lax.dot_general(part, low, dims, preferred_element_type=jnp.float32)
+        if ch:
+            store(ch - 1, lag)
+        part, lag = following, fresh
+    store(chans - 1, lag)
     for copy in copies:
         copy.wait()
 

time: 59.3 us -> 59.1 us (level)
  no operation moved by 1% of the time
where the time goes in v3:
time: 59.1 us; the launch traced here: 58.9 us
  blocking collectives  54.3 us (92%)
  Pallas kernels  4.56 us (8%)
    all_to_all x1, blocking collectives, shards(): cross = lax.all_to_all(cross, axes, 0, 0, tiled=True)  29.3 us
    all_to_all x1, blocking collectives, shards(): mine = lax.all_to_all(packed, axes, 0, 0, tiled=True)  25 us
    pallas_call x3, Pallas kernels, call(): pl.pallas_call(kernel, out_shape=out_shape, in_specs=[pl.BlockSpec(memory...  4.56 us

profile of v3, /device:TPU:1, one launch (start us, length us, event | category | flops | bytes accessed | tf_op | source)
XLA Modules:
  0.0 58.9 jit_solution(14471072632301020343)
XLA Ops:
  0.0 1.6 %shard_map.37 = bf16[32,5,16,128]{3,2,1,0:T(8,128)(2,1)S(1)} custom-call(bf16[16,80,256]{2,1,0:T(8,128)(2,1)} %bitcast.3), custom_call_target="tpu_custom_call" | custom-call | tf_op jit(solution)/shard_map/pallas_call | solution.py:226
  1.6 25.0 %all_to_all.10.in_ref = bf16[32,5,16,128]{3,2,1,0:T(8,128)(2,1)S(1)} all-to-all(bf16[32,5,16,128]{3,2,1,0:T(8,128)(2,1)S(1)} %shard_map.37), channel_id=1, replica_groups=mesh['outer'=4,'inner'=4,'day'=2] {'day','inner','outer'}, dimensions={0} | all-to-all | bytes 1310720 | tf_op jit(solution)/shard_map/all_to_all | solution.py:257
  26.6 0.0 copy-start
  26.6 0.0 copy-start.1
  26.6 0.7 %shard_map.38 = bf16[32,8,16,128]{3,2,1,0:T(8,128)(2,1)S(1)} custom-call(bf16[32,5,16,128]{3,2,1,0:T(8,128)(2,1)S(1)} %all_to_all.10.in_ref), custom_call_target="tpu_custom_call" | custom-call | tf_op jit(solution)/shard_map/pallas_call | solution.py:226
  27.3 29.3 %all_to_all.11 = bf16[32,8,16,128]{3,2,1,0:T(8,128)(2,1)S(1)} all-to-all(bf16[32,8,16,128]{3,2,1,0:T(8,128)(2,1)S(1)} %shard_map.38), channel_id=1, replica_groups=mesh['outer'=4,'inner'=4,'day'=2] {'day','inner','outer'}, dimensions={0} | all-to-all | bytes 2097152 | tf_op jit(solution)/shard_map/all_to_all | solution.py:266
  56.6 0.0 copy-done
  56.6 0.0 copy-done.1
  56.6 2.2 %shard_map.39 = f32[128,16,256]{2,1,0:T(8,128)} custom-call(bf16[4096,128]{1,0:T(8,128)(2,1)S(1)} %bitcast.2, bf16[256,256]{1,0:T(8,128)(2,1)S(1)} %copy-done.1, bf16[256,256]{1,0:T(8,128)(2,1)S(1)} %copy-done), custom_call_target="tpu_custom_call" | custom-call | tf_op jit(solution)/shard_map/pallas_call | solution.py:226
Async XLA Ops:
  26.6 30.1 %copy-start = (bf16[256,256]{1,0:T(8,128)(2,1)S(1)}, bf16[256,256]{1,0:T(8,128)(2,1)}, u32[]{:S(2)}) copy-start(bf16[256,256]{1,0:T(8,128)(2,1)} %constant.5.clone.low_ref) | copy-start | bytes 393220
  26.6 30.1 %copy-start.1 = (bf16[256,256]{1,0:T(8,128)(2,1)S(1)}, bf16[256,256]{1,0:T(8,128)(2,1)}, u32[]{:S(2)}) copy-start(bf16[256,256]{1,0:T(8,128)(2,1)} %constant.4.clone.high_ref) | copy-start | bytes 393220

commit v4 on v3

--- a/solution.py
+++ b/solution.py
@@ -10,8 +10,8 @@
 
 VMEM_LIMIT = 48 * 1024 * 1024
 PACK_VMEM_LIMIT = 53 * 1024 * 1024
-FETCHES = 2
-SENDS = 2
+FETCHES = (2, 4)
+SENDS = (2, 4)
 
 
 def freq_taper(bins):
@@ -91,12 +91,13 @@
     head = bins // 2
     size = (per_dev + 1) * chans
     stride = size + 1
-    fetches = arrived.shape[0]
+    fetches, pieces = arrived.shape
     batch = chans // fetches
     copies = []
-    for step in range(fetches):
-        part = pl.ds(step * batch, batch)
-        copies.append(pltpu.make_async_copy(spectra_ref.at[part], held_ref.at[part], arrived.at[step]))
+    for piece in range(fetches * pieces):
+        part = pl.ds(piece * (batch // pieces), batch // pieces)
+        place = divmod(piece, pieces)
+        copies.append(pltpu.make_async_copy(spectra_ref.at[part], held_ref.at[part], arrived.at[place]))
         copies[-1].start()
     freq = (lax.broadcasted_iota(jnp.int32, (1, width), 1) % bins).astype(jnp.float32)
     taper = 0.54 - 0.46 * jnp.cos(2.0 * jnp.pi * (freq + 0.5) / bins)
@@ -126,7 +127,8 @@
 
     ready = []
     for step in range(fetches):
-        copies[step].wait()
+        for copy in copies[step * pieces:(step + 1) * pieces]:
+            copy.wait()
         fresh = [(ch, whiten_channel(ch)) for ch in range(step * batch, (step + 1) * batch)]
         for ch, white in ready:
             place_channel(ch, white)
@@ -191,8 +193,9 @@
     depth = high_ref.shape[0]
     high, low = high_ref[...], low_ref[...]
     dims = (((0,), (0,)), ((), ()))
-    parts = sent.shape[0]
+    parts, pieces = sent.shape
     batch = chans // parts
+    run = out_ref.shape[0] // pieces
     stride = chans + 1
     for row in range(depth):
         rows_ref[pl.ds(row * stride, chans), :] = cross_ref[pl.ds(row * chans, chans), :].astype(jnp.float32)
@@ -205,9 +208,10 @@
         lag_ref[:, ch, :] = lag
         if (ch + 1) % batch == 0:
             step = ch // batch
-            done = pl.ds(step * batch, batch)
-            copies.append(pltpu.make_async_copy(lag_ref.at[:, done], out_ref.at[:, done], sent.at[step]))
-            copies[-1].start()
+            for piece in range(pieces):
+                place = (pl.ds(piece * run, run), pl.ds(step * batch, batch))
+                copies.append(pltpu.make_async_copy(lag_ref.at[place], out_ref.at[place], sent.at[step, piece]))
+                copies[-1].start()
 
     part, lag = load(0), None
     for ch in range(chans):
@@ -247,7 +251,7 @@
         [
             pltpu.VMEM((chans, windows, width), jnp.bfloat16),
             pltpu.VMEM((groups * ((per_dev + 1) * chans + 1), bins), jnp.float32),
-            pltpu.SemaphoreType.DMA((FETCHES,)),
+            pltpu.SemaphoreType.DMA(FETCHES),
         ],
         [pltpu.HBM],
         pltpu.VMEM,
@@ -271,7 +275,7 @@
         [
             pltpu.VMEM((width * (chans + 1), far), jnp.float32),
             pltpu.VMEM((far, chans, width), jnp.float32),
-            pltpu.SemaphoreType.DMA((SENDS,)),
+            pltpu.SemaphoreType.DMA(SENDS),
         ],
         [pltpu.VMEM] * 3,
         pltpu.HBM,

time: 59.1 us -> 59.2 us (level)
  no operation moved by 1% of the time
where the time goes in v4:
time: 59.2 us; the launch traced here: 59 us
  blocking collectives  54.3 us (92%)
  Pallas kernels  4.69 us (8%)
    all_to_all x1, blocking collectives, shards(): cross = lax.all_to_all(cross, axes, 0, 0, tiled=True)  29.3 us
    all_to_all x1, blocking collectives, shards(): mine = lax.all_to_all(packed, axes, 0, 0, tiled=True)  25 us
    pallas_call x3, Pallas kernels, call(): pl.pallas_call(kernel, out_shape=out_shape, in_specs=[pl.BlockSpec(memory...  4.69 us

profile of v4, /device:TPU:1, one launch (start us, length us, event | category | flops | bytes accessed | tf_op | source)
XLA Modules:
  0.0 59.0 jit_solution(6091523051375264792)
XLA Ops:
  0.0 1.7 %shard_map.37 = bf16[32,5,16,128]{3,2,1,0:T(8,128)(2,1)S(1)} custom-call(bf16[16,80,256]{2,1,0:T(8,128)(2,1)} %bitcast.3), custom_call_target="tpu_custom_call" | custom-call | tf_op jit(solution)/shard_map/pallas_call | solution.py:230
  1.7 25.0 %all_to_all.10.in_ref = bf16[32,5,16,128]{3,2,1,0:T(8,128)(2,1)S(1)} all-to-all(bf16[32,5,16,128]{3,2,1,0:T(8,128)(2,1)S(1)} %shard_map.37), channel_id=1, replica_groups=mesh['outer'=4,'inner'=4,'day'=2] {'day','inner','outer'}, dimensions={0} | all-to-all | bytes 1310720 | tf_op jit(solution)/shard_map/all_to_all | solution.py:261
  26.6 0.0 copy-start
  26.6 0.0 copy-start.1
  26.7 0.7 %shard_map.38 = bf16[32,8,16,128]{3,2,1,0:T(8,128)(2,1)S(1)} custom-call(bf16[32,5,16,128]{3,2,1,0:T(8,128)(2,1)S(1)} %all_to_all.10.in_ref), custom_call_target="tpu_custom_call" | custom-call | tf_op jit(solution)/shard_map/pallas_call | solution.py:230
  27.4 29.3 %all_to_all.11 = bf16[32,8,16,128]{3,2,1,0:T(8,128)(2,1)S(1)} all-to-all(bf16[32,8,16,128]{3,2,1,0:T(8,128)(2,1)S(1)} %shard_map.38), channel_id=1, replica_groups=mesh['outer'=4,'inner'=4,'day'=2] {'day','inner','outer'}, dimensions={0} | all-to-all | bytes 2097152 | tf_op jit(solution)/shard_map/all_to_all | solution.py:270
  56.7 0.0 copy-done
  56.7 0.0 copy-done.1
  56.7 2.3 %shard_map.39 = f32[128,16,256]{2,1,0:T(8,128)} custom-call(bf16[4096,128]{1,0:T(8,128)(2,1)S(1)} %bitcast.2, bf16[256,256]{1,0:T(8,128)(2,1)S(1)} %copy-done.1, bf16[256,256]{1,0:T(8,128)(2,1)S(1)} %copy-done), custom_call_target="tpu_custom_call" | custom-call | tf_op jit(solution)/shard_map/pallas_call | solution.py:230
Async XLA Ops:
  26.6 30.1 %copy-start = (bf16[256,256]{1,0:T(8,128)(2,1)S(1)}, bf16[256,256]{1,0:T(8,128)(2,1)}, u32[]{:S(2)}) copy-start(bf16[256,256]{1,0:T(8,128)(2,1)} %constant.5.clone.low_ref) | copy-start | bytes 393220
  26.6 30.1 %copy-start.1 = (bf16[256,256]{1,0:T(8,128)(2,1)S(1)}, bf16[256,256]{1,0:T(8,128)(2,1)}, u32[]{:S(2)}) copy-start(bf16[256,256]{1,0:T(8,128)(2,1)} %constant.4.clone.high_ref) | copy-start | bytes 393220

commit v5 on v3

--- a/solution.py
+++ b/solution.py
@@ -189,8 +189,7 @@
 def lags_kernel(cross_ref, high_ref, low_ref, out_ref, rows_ref, lag_ref, sent):
     chans = out_ref.shape[1]
     depth = high_ref.shape[0]
-    high, low = high_ref[...], low_ref[...]
-    dims = (((0,), (0,)), ((), ()))
+    table = jnp.concatenate([high_ref[...], low_ref[...]], axis=0)
     parts = sent.shape[0]
     batch = chans // parts
     stride = chans + 1
@@ -199,7 +198,8 @@
     copies = []
 
     def load(ch):
-        return rows_ref[pl.ds(ch, depth, stride=stride), :].astype(jnp.bfloat16)
+        part = rows_ref[pl.ds(ch, depth, stride=stride), :].astype(jnp.bfloat16).T
+        return jnp.concatenate([part, part], axis=1)
 
     def store(ch, lag):
         lag_ref[:, ch, :] = lag
@@ -212,8 +212,7 @@
     part, lag = load(0), None
     for ch in range(chans):
         following = load(ch + 1) if ch + 1 < chans else None
-        fresh = lax.dot_general(part, high, dims, preferred_element_type=jnp.float32)
-        fresh = fresh + lax.dot_general(part, low, dims, preferred_element_type=jnp.float32)
+        fresh = jnp.dot(part, table, preferred_element_type=jnp.float32)
         if ch:
             store(ch - 1, lag)
         part, lag = following, fresh

time: 59.1 us -> 59.1 us (level)
  no operation moved by 1% of the time
where the time goes in v5:
time: 59.1 us; the launch traced here: 58.9 us
  blocking collectives  54.3 us (92%)
  Pallas kernels  4.56 us (8%)
    all_to_all x1, blocking collectives, shards(): cross = lax.all_to_all(cross, axes, 0, 0, tiled=True)  29.3 us
    all_to_all x1, blocking collectives, shards(): mine = lax.all_to_all(packed, axes, 0, 0, tiled=True)  25 us
    pallas_call x3, Pallas kernels, call(): pl.pallas_call(kernel, out_shape=out_shape, in_specs=[pl.BlockSpec(memory...  4.56 us

profile of v5, /device:TPU:1, one launch (start us, length us, event | category | flops | bytes accessed | tf_op | source)
XLA Modules:
  0.0 58.9 jit_solution(5660952480330510921)
XLA Ops:
  0.0 1.6 %shard_map.37 = bf16[32,5,16,128]{3,2,1,0:T(8,128)(2,1)S(1)} custom-call(bf16[16,80,256]{2,1,0:T(8,128)(2,1)} %bitcast.3), custom_call_target="tpu_custom_call" | custom-call | tf_op jit(solution)/shard_map/pallas_call | solution.py:225
  1.6 25.0 %all_to_all.10.in_ref = bf16[32,5,16,128]{3,2,1,0:T(8,128)(2,1)S(1)} all-to-all(bf16[32,5,16,128]{3,2,1,0:T(8,128)(2,1)S(1)} %shard_map.37), channel_id=1, replica_groups=mesh['outer'=4,'inner'=4,'day'=2] {'day','inner','outer'}, dimensions={0} | all-to-all | bytes 1310720 | tf_op jit(solution)/shard_map/all_to_all | solution.py:256
  26.6 0.0 copy-start
  26.6 0.0 copy-start.1
  26.6 0.7 %shard_map.38 = bf16[32,8,16,128]{3,2,1,0:T(8,128)(2,1)S(1)} custom-call(bf16[32,5,16,128]{3,2,1,0:T(8,128)(2,1)S(1)} %all_to_all.10.in_ref), custom_call_target="tpu_custom_call" | custom-call | tf_op jit(solution)/shard_map/pallas_call | solution.py:225
  27.3 29.3 %all_to_all.11 = bf16[32,8,16,128]{3,2,1,0:T(8,128)(2,1)S(1)} all-to-all(bf16[32,8,16,128]{3,2,1,0:T(8,128)(2,1)S(1)} %shard_map.38), channel_id=1, replica_groups=mesh['outer'=4,'inner'=4,'day'=2] {'day','inner','outer'}, dimensions={0} | all-to-all | bytes 2097152 | tf_op jit(solution)/shard_map/all_to_all | solution.py:265
  56.6 0.0 copy-done
  56.6 0.0 copy-done.1
  56.6 2.2 %shard_map.39 = f32[128,16,256]{2,1,0:T(8,128)} custom-call(bf16[4096,128]{1,0:T(8,128)(2,1)S(1)} %bitcast.2, bf16[256,256]{1,0:T(8,128)(2,1)S(1)} %copy-done.1, bf16[256,256]{1,0:T(8,128)(2,1)S(1)} %copy-done), custom_call_target="tpu_custom_call" | custom-call | tf_op jit(solution)/shard_map/pallas_call | solution.py:225
Async XLA Ops:
  26.6 30.1 %copy-start = (bf16[256,256]{1,0:T(8,128)(2,1)S(1)}, bf16[256,256]{1,0:T(8,128)(2,1)}, u32[]{:S(2)}) copy-start(bf16[256,256]{1,0:T(8,128)(2,1)} %constant.5.clone.low_ref) | copy-start | bytes 393220
  26.6 30.1 %copy-start.1 = (bf16[256,256]{1,0:T(8,128)(2,1)S(1)}, bf16[256,256]{1,0:T(8,128)(2,1)}, u32[]{:S(2)}) copy-start(bf16[256,256]{1,0:T(8,128)(2,1)} %constant.4.clone.high_ref) | copy-start | bytes 393220

commit v6 on v1

--- a/solution.py
+++ b/solution.py
@@ -10,8 +10,8 @@
 
 VMEM_LIMIT = 48 * 1024 * 1024
 PACK_VMEM_LIMIT = 53 * 1024 * 1024
-FETCHES = 4
-SENDS = 2
+FETCHES = 2
+SENDS = (2, 2)
 
 
 def freq_taper(bins):
@@ -133,9 +133,10 @@
         ready = fresh
     for ch, white in ready:
         place_channel(ch, white)
-    for group in range(groups):
-        rows = rows_ref[pl.ds(group * stride, size), :]
-        out_ref[group] = rows.astype(jnp.bfloat16).reshape(out_ref.shape[1:])
+    for first in range(0, groups, 4):
+        rows = [rows_ref[pl.ds(group * stride, size), :].astype(jnp.bfloat16) for group in range(first, first + 4)]
+        for place, part in enumerate(rows):
+            out_ref[first + place] = part.reshape(out_ref.shape[1:])
 
 
 def swap_parts(rows, half):
@@ -188,12 +189,11 @@
 def lags_kernel(cross_ref, high_ref, low_ref, out_ref, rows_ref, lag_ref, sent):
     chans = out_ref.shape[1]
     depth = high_ref.shape[0]
-    high, low = high_ref[...], low_ref[...]
-    dims = (((0,), (0,)), ((), ()))
-    parts = sent.shape[0]
+    table = jnp.concatenate([high_ref[...], low_ref[...]], axis=0)
+    parts, pieces = sent.shape
     batch = chans // parts
+    run = out_ref.shape[0] // pieces
     stride = batch + 1
-    share = depth // batch
 
     def fill(step, rows):
         for row in rows:
@@ -203,16 +203,21 @@
     fill(0, range(depth))
     copies = []
     for step in range(parts):
+        turned = []
         for place in range(batch):
-            part = rows_ref[step, pl.ds(place, depth, stride=stride), :].astype(jnp.bfloat16)
+            part = rows_ref[step, pl.ds(place, depth, stride=stride), :].astype(jnp.bfloat16).T
+            turned.append(jnp.concatenate([part, part], axis=1))
+        for piece in range(pieces):
+            done = pl.ds(piece * run, run)
+            for place, part in enumerate(turned):
+                lag = jnp.dot(part[piece * run:(piece + 1) * run], table, preferred_element_type=jnp.float32)
+                lag_ref[done, step * batch + place, :] = lag
+            place = (done, pl.ds(step * batch, batch))
+            copies.append(pltpu.make_async_copy(lag_ref.at[place], out_ref.at[place], sent.at[step, piece]))
+            copies[-1].start()
             if step + 1 < parts:
-                fill(step + 1, range(place * share, (place + 1) * share))
-            lag = lax.dot_general(part, high, dims, preferred_element_type=jnp.float32)
-            lag = lag + lax.dot_general(part, low, dims, preferred_element_type=jnp.float32)
-            lag_ref[:, step * batch + place, :] = lag
-        done = pl.ds(step * batch, batch)
-        copies.append(pltpu.make_async_copy(lag_ref.at[:, done], out_ref.at[:, done], sent.at[step]))
-        copies[-1].start()
+                share = depth // pieces
+                fill(step + 1, range(piece * share, (piece + 1) * share))
     for copy in copies:
         copy.wait()
 
@@ -264,9 +269,9 @@
         lags_kernel,
         jax.ShapeDtypeStruct((far, chans, width), jnp.float32),
         [
-            pltpu.VMEM((SENDS, width * (chans // SENDS + 1), far), jnp.float32),
+            pltpu.VMEM((SENDS[0], width * (chans // SENDS[0] + 1), far), jnp.float32),
             pltpu.VMEM((far, chans, width), jnp.float32),
-            pltpu.SemaphoreType.DMA((SENDS,)),
+            pltpu.SemaphoreType.DMA(SENDS),
         ],
         [pltpu.VMEM] * 3,
         pltpu.HBM,

time: 59.2 us -> 59.6 us (level)
  no operation moved by 1% of the time
where the time goes in v6:
time: 59.6 us; the launch traced here: 59.4 us
  blocking collectives  54.3 us (91%)
  Pallas kernels  5.08 us (9%)
    all_to_all x1, blocking collectives, shards(): cross = lax.all_to_all(cross, axes, 0, 0, tiled=True)  29.3 us
    all_to_all x1, blocking collectives, shards(): mine = lax.all_to_all(packed, axes, 0, 0, tiled=True)  25 us
    pallas_call x3, Pallas kernels, call(): pl.pallas_call(kernel, out_shape=out_shape, in_specs=[pl.BlockSpec(memory...  5.08 us

profile of v6, /device:TPU:1, one launch (start us, length us, event | category | flops | bytes accessed | tf_op | source)
XLA Modules:
  0.0 59.4 jit_solution(16419466577034769164)
XLA Ops:
  0.0 1.6 %shard_map.37 = bf16[32,5,16,128]{3,2,1,0:T(8,128)(2,1)S(1)} custom-call(bf16[16,80,256]{2,1,0:T(8,128)(2,1)} %bitcast.3), custom_call_target="tpu_custom_call" | custom-call | tf_op jit(solution)/shard_map/pallas_call | solution.py:226
  1.6 25.0 %all_to_all.10.in_ref = bf16[32,5,16,128]{3,2,1,0:T(8,128)(2,1)S(1)} all-to-all(bf16[32,5,16,128]{3,2,1,0:T(8,128)(2,1)S(1)} %shard_map.37), channel_id=1, replica_groups=mesh['outer'=4,'inner'=4,'day'=2] {'day','inner','outer'}, dimensions={0} | all-to-all | bytes 1310720 | tf_op jit(solution)/shard_map/all_to_all | solution.py:257
  26.6 0.0 copy-start
  26.6 0.0 copy-start.1
  26.6 0.7 %shard_map.38 = bf16[32,8,16,128]{3,2,1,0:T(8,128)(2,1)S(1)} custom-call(bf16[32,5,16,128]{3,2,1,0:T(8,128)(2,1)S(1)} %all_to_all.10.in_ref), custom_call_target="tpu_custom_call" | custom-call | tf_op jit(solution)/shard_map/pallas_call | solution.py:226
  27.3 29.3 %all_to_all.11 = bf16[32,8,16,128]{3,2,1,0:T(8,128)(2,1)S(1)} all-to-all(bf16[32,8,16,128]{3,2,1,0:T(8,128)(2,1)S(1)} %shard_map.38), channel_id=1, replica_groups=mesh['outer'=4,'inner'=4,'day'=2] {'day','inner','outer'}, dimensions={0} | all-to-all | bytes 2097152 | tf_op jit(solution)/shard_map/all_to_all | solution.py:266
  56.6 0.0 copy-done
  56.6 0.0 copy-done.1
  56.6 2.8 %shard_map.39 = f32[128,16,256]{2,1,0:T(8,128)} custom-call(bf16[4096,128]{1,0:T(8,128)(2,1)S(1)} %bitcast.2, bf16[256,256]{1,0:T(8,128)(2,1)S(1)} %copy-done.1, bf16[256,256]{1,0:T(8,128)(2,1)S(1)} %copy-done), custom_call_target="tpu_custom_call" | custom-call | tf_op jit(solution)/shard_map/pallas_call | solution.py:226
Async XLA Ops:
  26.6 30.1 %copy-start = (bf16[256,256]{1,0:T(8,128)(2,1)S(1)}, bf16[256,256]{1,0:T(8,128)(2,1)}, u32[]{:S(2)}) copy-start(bf16[256,256]{1,0:T(8,128)(2,1)} %constant.5.clone.low_ref) | copy-start | bytes 393220
  26.6 30.1 %copy-start.1 = (bf16[256,256]{1,0:T(8,128)(2,1)S(1)}, bf16[256,256]{1,0:T(8,128)(2,1)}, u32[]{:S(2)}) copy-start(bf16[256,256]{1,0:T(8,128)(2,1)} %constant.4.clone.high_ref) | copy-start | bytes 393220

commit v7 on v5

--- a/solution.py
+++ b/solution.py
@@ -12,6 +12,7 @@
 PACK_VMEM_LIMIT = 53 * 1024 * 1024
 FETCHES = 2
 SENDS = 2
+TALL = 2
 
 
 def freq_taper(bins):
@@ -187,7 +188,7 @@
 
 
 def lags_kernel(cross_ref, high_ref, low_ref, out_ref, rows_ref, lag_ref, sent):
-    chans = out_ref.shape[1]
+    far, chans, _ = out_ref.shape
     depth = high_ref.shape[0]
     table = jnp.concatenate([high_ref[...], low_ref[...]], axis=0)
     parts = sent.shape[0]
@@ -197,26 +198,28 @@
         rows_ref[pl.ds(row * stride, chans), :] = cross_ref[pl.ds(row * chans, chans), :].astype(jnp.float32)
     copies = []
 
-    def load(ch):
-        part = rows_ref[pl.ds(ch, depth, stride=stride), :].astype(jnp.bfloat16).T
+    def load(first):
+        part = [rows_ref[pl.ds(ch, depth, stride=stride), :].astype(jnp.bfloat16).T for ch in range(first, first + TALL)]
+        part = jnp.concatenate(part, axis=0)
         return jnp.concatenate([part, part], axis=1)
 
-    def store(ch, lag):
-        lag_ref[:, ch, :] = lag
-        if (ch + 1) % batch == 0:
-            step = ch // batch
+    def store(first, lag):
+        for place in range(TALL):
+            lag_ref[:, first + place, :] = lag[place * far:(place + 1) * far]
+        if (first + TALL) % batch == 0:
+            step = first // batch
             done = pl.ds(step * batch, batch)
             copies.append(pltpu.make_async_copy(lag_ref.at[:, done], out_ref.at[:, done], sent.at[step]))
             copies[-1].start()
 
     part, lag = load(0), None
-    for ch in range(chans):
-        following = load(ch + 1) if ch + 1 < chans else None
+    for ch in range(0, chans, TALL):
+        following = load(ch + TALL) if ch + TALL < chans else None
         fresh = jnp.dot(part, table, preferred_element_type=jnp.float32)
         if ch:
-            store(ch - 1, lag)
+            store(ch - TALL, lag)
         part, lag = following, fresh
-    store(chans - 1, lag)
+    store(chans - TALL, lag)
     for copy in copies:
         copy.wait()
 

time: 59.1 us -> 59.1 us (level)
  no operation moved by 1% of the time
where the time goes in v7:
time: 59.1 us; the launch traced here: 58.9 us
  blocking collectives  54.3 us (92%)
  Pallas kernels  4.59 us (8%)
    all_to_all x1, blocking collectives, shards(): cross = lax.all_to_all(cross, axes, 0, 0, tiled=True)  29.3 us
    all_to_all x1, blocking collectives, shards(): mine = lax.all_to_all(packed, axes, 0, 0, tiled=True)  25 us
    pallas_call x3, Pallas kernels, call(): pl.pallas_call(kernel, out_shape=out_shape, in_specs=[pl.BlockSpec(memory...  4.59 us

profile of v7, /device:TPU:1, one launch (start us, length us, event | category | flops | bytes accessed | tf_op | source)
XLA Modules:
  0.0 58.9 jit_solution(14750515453308335116)
XLA Ops:
  0.0 1.6 %shard_map.37 = bf16[32,5,16,128]{3,2,1,0:T(8,128)(2,1)S(1)} custom-call(bf16[16,80,256]{2,1,0:T(8,128)(2,1)} %bitcast.3), custom_call_target="tpu_custom_call" | custom-call | tf_op jit(solution)/shard_map/pallas_call | solution.py:228
  1.6 25.0 %all_to_all.10.in_ref = bf16[32,5,16,128]{3,2,1,0:T(8,128)(2,1)S(1)} all-to-all(bf16[32,5,16,128]{3,2,1,0:T(8,128)(2,1)S(1)} %shard_map.37), channel_id=1, replica_groups=mesh['outer'=4,'inner'=4,'day'=2] {'day','inner','outer'}, dimensions={0} | all-to-all | bytes 1310720 | tf_op jit(solution)/shard_map/all_to_all | solution.py:259
  26.6 0.0 copy-start
  26.6 0.0 copy-start.1
  26.6 0.7 %shard_map.38 = bf16[32,8,16,128]{3,2,1,0:T(8,128)(2,1)S(1)} custom-call(bf16[32,5,16,128]{3,2,1,0:T(8,128)(2,1)S(1)} %all_to_all.10.in_ref), custom_call_target="tpu_custom_call" | custom-call | tf_op jit(solution)/shard_map/pallas_call | solution.py:228
  27.3 29.3 %all_to_all.11 = bf16[32,8,16,128]{3,2,1,0:T(8,128)(2,1)S(1)} all-to-all(bf16[32,8,16,128]{3,2,1,0:T(8,128)(2,1)S(1)} %shard_map.38), channel_id=1, replica_groups=mesh['outer'=4,'inner'=4,'day'=2] {'day','inner','outer'}, dimensions={0} | all-to-all | bytes 2097152 | tf_op jit(solution)/shard_map/all_to_all | solution.py:268
  56.6 0.0 copy-done
  56.6 0.0 copy-done.1
  56.6 2.3 %shard_map.39 = f32[128,16,256]{2,1,0:T(8,128)} custom-call(bf16[4096,128]{1,0:T(8,128)(2,1)S(1)} %bitcast.2, bf16[256,256]{1,0:T(8,128)(2,1)S(1)} %copy-done.1, bf16[256,256]{1,0:T(8,128)(2,1)S(1)} %copy-done), custom_call_target="tpu_custom_call" | custom-call | tf_op jit(solution)/shard_map/pallas_call | solution.py:228
Async XLA Ops:
  26.6 30.1 %copy-start = (bf16[256,256]{1,0:T(8,128)(2,1)S(1)}, bf16[256,256]{1,0:T(8,128)(2,1)}, u32[]{:S(2)}) copy-start(bf16[256,256]{1,0:T(8,128)(2,1)} %constant.5.clone.low_ref) | copy-start | bytes 393220
  26.6 30.1 %copy-start.1 = (bf16[256,256]{1,0:T(8,128)(2,1)S(1)}, bf16[256,256]{1,0:T(8,128)(2,1)}, u32[]{:S(2)}) copy-start(bf16[256,256]{1,0:T(8,128)(2,1)} %constant.4.clone.high_ref) | copy-start | bytes 393220

commit v8 on v3

--- a/solution.py
+++ b/solution.py
@@ -130,11 +130,14 @@
         fresh = [(ch, whiten_channel(ch)) for ch in range(step * batch, (step + 1) * batch)]
         for ch, white in ready:
             place_channel(ch, white)
-        ready = fresh
+        early = batch // 2 if step + 1 < fetches else 0
+        for ch, white in fresh[:early]:
+            place_channel(ch, white)
+        ready = fresh[early:]
     for ch, white in ready:
         place_channel(ch, white)
-    for first in range(0, groups, 4):
-        rows = [rows_ref[pl.ds(group * stride, size), :].astype(jnp.bfloat16) for group in range(first, first + 4)]
+    for first in range(0, groups, 8):
+        rows = [rows_ref[pl.ds(group * stride, size), :].astype(jnp.bfloat16) for group in range(first, first + 8)]
         for place, part in enumerate(rows):
             out_ref[first + place] = part.reshape(out_ref.shape[1:])
 

time: 59.1 us -> 59.1 us (level)
  no operation moved by 1% of the time
where the time goes in v8:
time: 59.1 us; the launch traced here: 58.9 us
  blocking collectives  54.3 us (92%)
  Pallas kernels  4.61 us (8%)
    all_to_all x1, blocking collectives, shards(): cross = lax.all_to_all(cross, axes, 0, 0, tiled=True)  29.3 us
    all_to_all x1, blocking collectives, shards(): mine = lax.all_to_all(packed, axes, 0, 0, tiled=True)  25 us
    pallas_call x3, Pallas kernels, call(): pl.pallas_call(kernel, out_shape=out_shape, in_specs=[pl.BlockSpec(memory...  4.61 us

profile of v8, /device:TPU:1, one launch (start us, length us, event | category | flops | bytes accessed | tf_op | source)
XLA Modules:
  0.0 58.9 jit_solution(1227673344712246190)
XLA Ops:
  0.0 1.6 %shard_map.37 = bf16[32,5,16,128]{3,2,1,0:T(8,128)(2,1)S(1)} custom-call(bf16[16,80,256]{2,1,0:T(8,128)(2,1)} %bitcast.3), custom_call_target="tpu_custom_call" | custom-call | tf_op jit(solution)/shard_map/pallas_call | solution.py:229
  1.6 25.0 %all_to_all.10.in_ref = bf16[32,5,16,128]{3,2,1,0:T(8,128)(2,1)S(1)} all-to-all(bf16[32,5,16,128]{3,2,1,0:T(8,128)(2,1)S(1)} %shard_map.37), channel_id=1, replica_groups=mesh['outer'=4,'inner'=4,'day'=2] {'day','inner','outer'}, dimensions={0} | all-to-all | bytes 1310720 | tf_op jit(solution)/shard_map/all_to_all | solution.py:260
  26.6 0.0 copy-start
  26.6 0.0 copy-start.1
  26.6 0.7 %shard_map.38 = bf16[32,8,16,128]{3,2,1,0:T(8,128)(2,1)S(1)} custom-call(bf16[32,5,16,128]{3,2,1,0:T(8,128)(2,1)S(1)} %all_to_all.10.in_ref), custom_call_target="tpu_custom_call" | custom-call | tf_op jit(solution)/shard_map/pallas_call | solution.py:229
  27.4 29.3 %all_to_all.11 = bf16[32,8,16,128]{3,2,1,0:T(8,128)(2,1)S(1)} all-to-all(bf16[32,8,16,128]{3,2,1,0:T(8,128)(2,1)S(1)} %shard_map.38), channel_id=1, replica_groups=mesh['outer'=4,'inner'=4,'day'=2] {'day','inner','outer'}, dimensions={0} | all-to-all | bytes 2097152 | tf_op jit(solution)/shard_map/all_to_all | solution.py:269
  56.7 0.0 copy-done
  56.7 0.0 copy-done.1
  56.7 2.2 %shard_map.39 = f32[128,16,256]{2,1,0:T(8,128)} custom-call(bf16[4096,128]{1,0:T(8,128)(2,1)S(1)} %bitcast.2, bf16[256,256]{1,0:T(8,128)(2,1)S(1)} %copy-done.1, bf16[256,256]{1,0:T(8,128)(2,1)S(1)} %copy-done), custom_call_target="tpu_custom_call" | custom-call | tf_op jit(solution)/shard_map/pallas_call | solution.py:229
Async XLA Ops:
  26.6 30.1 %copy-start = (bf16[256,256]{1,0:T(8,128)(2,1)S(1)}, bf16[256,256]{1,0:T(8,128)(2,1)}, u32[]{:S(2)}) copy-start(bf16[256,256]{1,0:T(8,128)(2,1)} %constant.5.clone.low_ref) | copy-start | bytes 393220
  26.6 30.1 %copy-start.1 = (bf16[256,256]{1,0:T(8,128)(2,1)S(1)}, bf16[256,256]{1,0:T(8,128)(2,1)}, u32[]{:S(2)}) copy-start(bf16[256,256]{1,0:T(8,128)(2,1)} %constant.4.clone.high_ref) | copy-start | bytes 393220

commit v9 on v3

--- a/solution.py
+++ b/solution.py
@@ -162,21 +162,17 @@
 
     tails = [rows(day, per_dev) for day in range(days)]
     tails_swapped = [swap_parts(tail, narrow) for tail in tails]
-    far_tail = jnp.concatenate(tails, axis=1)
     lane = lax.broadcasted_iota(jnp.int32, (2 * total, lanes), 1) // (2 * narrow)
     dims = (((1,), (1,)), ((), ()))
     for slot in range(per_dev):
         mains = [rows(day, slot) for day in range(days)]
-        far_main = jnp.concatenate(mains, axis=1)
+        far_rows = jnp.concatenate(mains + tails, axis=1)
         turned = [swap_parts(m, lanes // 2) for m in mains]
         near_main = [jnp.concatenate(pair, axis=0) for pair in zip(mains, turned)]
         near_tail = [jnp.concatenate(pair, axis=0) for pair in zip(tails, tails_swapped)]
         near_tail = [jnp.where(lane == slot, t, jnp.zeros_like(t)) for t in near_tail]
-        cross = lax.dot_general(
-            jnp.concatenate(near_main, axis=1), far_main, dims, preferred_element_type=jnp.float32
-        ) + lax.dot_general(
-            jnp.concatenate(near_tail, axis=1), far_tail, dims, preferred_element_type=jnp.float32
-        )
+        near = jnp.concatenate(near_main + near_tail, axis=1)
+        cross = lax.dot_general(near, far_rows, dims, preferred_element_type=jnp.float32)
         cross = cross.astype(out_ref.dtype)
         for kind in range(2):
             for block in range(blocks):

time: 59.1 us -> 59.1 us (level)
  no operation moved by 1% of the time
where the time goes in v9:
time: 59.1 us; the launch traced here: 58.9 us
  blocking collectives  54.3 us (92%)
  Pallas kernels  4.56 us (8%)
    all_to_all x1, blocking collectives, shards(): cross = lax.all_to_all(cross, axes, 0, 0, tiled=True)  29.3 us
    all_to_all x1, blocking collectives, shards(): mine = lax.all_to_all(packed, axes, 0, 0, tiled=True)  25 us
    pallas_call x3, Pallas kernels, call(): pl.pallas_call(kernel, out_shape=out_shape, in_specs=[pl.BlockSpec(memory...  4.56 us

profile of v9, /device:TPU:1, one launch (start us, length us, event | category | flops | bytes accessed | tf_op | source)
XLA Modules:
  0.0 58.9 jit_solution(12949289556337493710)
XLA Ops:
  0.0 1.6 %shard_map.37 = bf16[32,5,16,128]{3,2,1,0:T(8,128)(2,1)S(1)} custom-call(bf16[16,80,256]{2,1,0:T(8,128)(2,1)} %bitcast.3), custom_call_target="tpu_custom_call" | custom-call | tf_op jit(solution)/shard_map/pallas_call | solution.py:222
  1.6 25.0 %all_to_all.10.in_ref = bf16[32,5,16,128]{3,2,1,0:T(8,128)(2,1)S(1)} all-to-all(bf16[32,5,16,128]{3,2,1,0:T(8,128)(2,1)S(1)} %shard_map.37), channel_id=1, replica_groups=mesh['outer'=4,'inner'=4,'day'=2] {'day','inner','outer'}, dimensions={0} | all-to-all | bytes 1310720 | tf_op jit(solution)/shard_map/all_to_all | solution.py:253
  26.6 0.0 copy-start
  26.6 0.0 copy-start.1
  26.6 0.8 %shard_map.38 = bf16[32,8,16,128]{3,2,1,0:T(8,128)(2,1)S(1)} custom-call(bf16[32,5,16,128]{3,2,1,0:T(8,128)(2,1)S(1)} %all_to_all.10.in_ref), custom_call_target="tpu_custom_call" | custom-call | tf_op jit(solution)/shard_map/pallas_call | solution.py:222
  27.3 29.3 %all_to_all.11 = bf16[32,8,16,128]{3,2,1,0:T(8,128)(2,1)S(1)} all-to-all(bf16[32,8,16,128]{3,2,1,0:T(8,128)(2,1)S(1)} %shard_map.38), channel_id=1, replica_groups=mesh['outer'=4,'inner'=4,'day'=2] {'day','inner','outer'}, dimensions={0} | all-to-all | bytes 2097152 | tf_op jit(solution)/shard_map/all_to_all | solution.py:262
  56.6 0.0 copy-done
  56.6 0.0 copy-done.1
  56.6 2.2 %shard_map.39 = f32[128,16,256]{2,1,0:T(8,128)} custom-call(bf16[4096,128]{1,0:T(8,128)(2,1)S(1)} %bitcast.2, bf16[256,256]{1,0:T(8,128)(2,1)S(1)} %copy-done.1, bf16[256,256]{1,0:T(8,128)(2,1)S(1)} %copy-done), custom_call_target="tpu_custom_call" | custom-call | tf_op jit(solution)/shard_map/pallas_call | solution.py:222
Async XLA Ops:
  26.6 30.1 %copy-start = (bf16[256,256]{1,0:T(8,128)(2,1)S(1)}, bf16[256,256]{1,0:T(8,128)(2,1)}, u32[]{:S(2)}) copy-start(bf16[256,256]{1,0:T(8,128)(2,1)} %constant.5.clone.low_ref) | copy-start | bytes 393220
  26.6 30.1 %copy-start.1 = (bf16[256,256]{1,0:T(8,128)(2,1)S(1)}, bf16[256,256]{1,0:T(8,128)(2,1)}, u32[]{:S(2)}) copy-start(bf16[256,256]{1,0:T(8,128)(2,1)} %constant.4.clone.high_ref) | copy-start | bytes 393220

commit v10 on v9

--- a/solution.py
+++ b/solution.py
@@ -162,15 +162,15 @@
 
     tails = [rows(day, per_dev) for day in range(days)]
     tails_swapped = [swap_parts(tail, narrow) for tail in tails]
-    lane = lax.broadcasted_iota(jnp.int32, (2 * total, lanes), 1) // (2 * narrow)
+    near_tail = [jnp.concatenate(pair, axis=0) for pair in zip(tails, tails_swapped)]
+    lane = lax.broadcasted_iota(jnp.int32, (total, lanes), 1) // (2 * narrow)
     dims = (((1,), (1,)), ((), ()))
     for slot in range(per_dev):
         mains = [rows(day, slot) for day in range(days)]
-        far_rows = jnp.concatenate(mains + tails, axis=1)
+        chosen = [jnp.where(lane == slot, t, jnp.zeros_like(t)) for t in tails]
+        far_rows = jnp.concatenate(mains + chosen, axis=1)
         turned = [swap_parts(m, lanes // 2) for m in mains]
         near_main = [jnp.concatenate(pair, axis=0) for pair in zip(mains, turned)]
-        near_tail = [jnp.concatenate(pair, axis=0) for pair in zip(tails, tails_swapped)]
-        near_tail = [jnp.where(lane == slot, t, jnp.zeros_like(t)) for t in near_tail]
         near = jnp.concatenate(near_main + near_tail, axis=1)
         cross = lax.dot_general(near, far_rows, dims, preferred_element_type=jnp.float32)
         cross = cross.astype(out_ref.dtype)

time: 59.1 us -> 59.1 us (level)
  no operation moved by 1% of the time
where the time goes in v10:
time: 59.1 us; the launch traced here: 58.9 us
  blocking collectives  54.3 us (92%)
  Pallas kernels  4.56 us (8%)
    all_to_all x1, blocking collectives, shards(): cross = lax.all_to_all(cross, axes, 0, 0, tiled=True)  29.3 us
    all_to_all x1, blocking collectives, shards(): mine = lax.all_to_all(packed, axes, 0, 0, tiled=True)  25 us
    pallas_call x3, Pallas kernels, call(): pl.pallas_call(kernel, out_shape=out_shape, in_specs=[pl.BlockSpec(memory...  4.56 us

profile of v10, /device:TPU:1, one launch (start us, length us, event | category | flops | bytes accessed | tf_op | source)
XLA Modules:
  0.0 58.9 jit_solution(15600736607799185548)
XLA Ops:
  0.0 1.6 %shard_map.37 = bf16[32,5,16,128]{3,2,1,0:T(8,128)(2,1)S(1)} custom-call(bf16[16,80,256]{2,1,0:T(8,128)(2,1)} %bitcast.3), custom_call_target="tpu_custom_call" | custom-call | tf_op jit(solution)/shard_map/pallas_call | solution.py:222
  1.6 25.0 %all_to_all.10.in_ref = bf16[32,5,16,128]{3,2,1,0:T(8,128)(2,1)S(1)} all-to-all(bf16[32,5,16,128]{3,2,1,0:T(8,128)(2,1)S(1)} %shard_map.37), channel_id=1, replica_groups=mesh['outer'=4,'inner'=4,'day'=2] {'day','inner','outer'}, dimensions={0} | all-to-all | bytes 1310720 | tf_op jit(solution)/shard_map/all_to_all | solution.py:253
  26.6 0.0 copy-start
  26.6 0.0 copy-start.1
  26.6 0.7 %shard_map.38 = bf16[32,8,16,128]{3,2,1,0:T(8,128)(2,1)S(1)} custom-call(bf16[32,5,16,128]{3,2,1,0:T(8,128)(2,1)S(1)} %all_to_all.10.in_ref), custom_call_target="tpu_custom_call" | custom-call | tf_op jit(solution)/shard_map/pallas_call | solution.py:222
  27.3 29.3 %all_to_all.11 = bf16[32,8,16,128]{3,2,1,0:T(8,128)(2,1)S(1)} all-to-all(bf16[32,8,16,128]{3,2,1,0:T(8,128)(2,1)S(1)} %shard_map.38), channel_id=1, replica_groups=mesh['outer'=4,'inner'=4,'day'=2] {'day','inner','outer'}, dimensions={0} | all-to-all | bytes 2097152 | tf_op jit(solution)/shard_map/all_to_all | solution.py:262
  56.6 0.0 copy-done
  56.6 0.0 copy-done.1
  56.6 2.2 %shard_map.39 = f32[128,16,256]{2,1,0:T(8,128)} custom-call(bf16[4096,128]{1,0:T(8,128)(2,1)S(1)} %bitcast.2, bf16[256,256]{1,0:T(8,128)(2,1)S(1)} %copy-done.1, bf16[256,256]{1,0:T(8,128)(2,1)S(1)} %copy-done), custom_call_target="tpu_custom_call" | custom-call | tf_op jit(solution)/shard_map/pallas_call | solution.py:222
Async XLA Ops:
  26.6 30.1 %copy-start = (bf16[256,256]{1,0:T(8,128)(2,1)S(1)}, bf16[256,256]{1,0:T(8,128)(2,1)}, u32[]{:S(2)}) copy-start(bf16[256,256]{1,0:T(8,128)(2,1)} %constant.5.clone.low_ref) | copy-start | bytes 393220
  26.6 30.1 %copy-start.1 = (bf16[256,256]{1,0:T(8,128)(2,1)S(1)}, bf16[256,256]{1,0:T(8,128)(2,1)}, u32[]{:S(2)}) copy-start(bf16[256,256]{1,0:T(8,128)(2,1)} %constant.4.clone.high_ref) | copy-start | bytes 393220

commit v11 on v3

--- a/solution.py
+++ b/solution.py
@@ -10,7 +10,7 @@
 
 VMEM_LIMIT = 48 * 1024 * 1024
 PACK_VMEM_LIMIT = 53 * 1024 * 1024
-FETCHES = 2
+FETCHES = 1
 SENDS = 2
 
 

time: 59.1 us -> 59.1 us (level)
  no operation moved by 1% of the time
where the time goes in v11:
time: 59.1 us; the launch traced here: 58.9 us
  blocking collectives  54.3 us (92%)
  Pallas kernels  4.62 us (8%)
    all_to_all x1, blocking collectives, shards(): cross = lax.all_to_all(cross, axes, 0, 0, tiled=True)  29.3 us
    all_to_all x1, blocking collectives, shards(): mine = lax.all_to_all(packed, axes, 0, 0, tiled=True)  25 us
    pallas_call x3, Pallas kernels, call(): pl.pallas_call(kernel, out_shape=out_shape, in_specs=[pl.BlockSpec(memory...  4.62 us

profile of v11, /device:TPU:1, one launch (start us, length us, event | category | flops | bytes accessed | tf_op | source)
XLA Modules:
  0.0 58.9 jit_solution(2379448344871672580)
XLA Ops:
  0.0 1.6 %shard_map.37 = bf16[32,5,16,128]{3,2,1,0:T(8,128)(2,1)S(1)} custom-call(bf16[16,80,256]{2,1,0:T(8,128)(2,1)} %bitcast.3), custom_call_target="tpu_custom_call" | custom-call | tf_op jit(solution)/shard_map/pallas_call | solution.py:226
  1.6 25.0 %all_to_all.10.in_ref = bf16[32,5,16,128]{3,2,1,0:T(8,128)(2,1)S(1)} all-to-all(bf16[32,5,16,128]{3,2,1,0:T(8,128)(2,1)S(1)} %shard_map.37), channel_id=1, replica_groups=mesh['outer'=4,'inner'=4,'day'=2] {'day','inner','outer'}, dimensions={0} | all-to-all | bytes 1310720 | tf_op jit(solution)/shard_map/all_to_all | solution.py:257
  26.6 0.0 copy-start
  26.6 0.0 copy-start.1
  26.6 0.7 %shard_map.38 = bf16[32,8,16,128]{3,2,1,0:T(8,128)(2,1)S(1)} custom-call(bf16[32,5,16,128]{3,2,1,0:T(8,128)(2,1)S(1)} %all_to_all.10.in_ref), custom_call_target="tpu_custom_call" | custom-call | tf_op jit(solution)/shard_map/pallas_call | solution.py:226
  27.4 29.3 %all_to_all.11 = bf16[32,8,16,128]{3,2,1,0:T(8,128)(2,1)S(1)} all-to-all(bf16[32,8,16,128]{3,2,1,0:T(8,128)(2,1)S(1)} %shard_map.38), channel_id=1, replica_groups=mesh['outer'=4,'inner'=4,'day'=2] {'day','inner','outer'}, dimensions={0} | all-to-all | bytes 2097152 | tf_op jit(solution)/shard_map/all_to_all | solution.py:266
  56.7 0.0 copy-done
  56.7 0.0 copy-done.1
  56.7 2.2 %shard_map.39 = f32[128,16,256]{2,1,0:T(8,128)} custom-call(bf16[4096,128]{1,0:T(8,128)(2,1)S(1)} %bitcast.2, bf16[256,256]{1,0:T(8,128)(2,1)S(1)} %copy-done.1, bf16[256,256]{1,0:T(8,128)(2,1)S(1)} %copy-done), custom_call_target="tpu_custom_call" | custom-call | tf_op jit(solution)/shard_map/pallas_call | solution.py:226
Async XLA Ops:
  26.6 30.1 %copy-start = (bf16[256,256]{1,0:T(8,128)(2,1)S(1)}, bf16[256,256]{1,0:T(8,128)(2,1)}, u32[]{:S(2)}) copy-start(bf16[256,256]{1,0:T(8,128)(2,1)} %constant.5.clone.low_ref) | copy-start | bytes 393220
  26.6 30.1 %copy-start.1 = (bf16[256,256]{1,0:T(8,128)(2,1)S(1)}, bf16[256,256]{1,0:T(8,128)(2,1)}, u32[]{:S(2)}) copy-start(bf16[256,256]{1,0:T(8,128)(2,1)} %constant.4.clone.high_ref) | copy-start | bytes 393220
